TPU v7x, 128 devices: a whole 4x4x4 slice. The times are simulated.
128 devices in a mesh: frames: 64 (over z, y, x_lo, core), dp: 2 (over x_hi).
Axes of the slice: x: 4 (x_hi: 2, x_lo: 2; x = x_hi * 2 + x_lo), y: 4, z: 4, core: 2. Of those that a mesh axis runs over, the one named last changes fastest.
Arguments:
- shifted: bfloat16 [2, 256, 16, 16, 640], P('dp', 'frames'), may hold values from -6 to 6
- out_grad: bfloat16 [2, 256, 16, 16, 640], P('dp', 'frames'), may hold values from -6 to 6
- conv_weight: bfloat16 [640, 5760], P('frames'), may hold values from -0.078125 to 0.078125
- norm_gain: float32 [640], replicated, may hold values from 0.5 to 2
- norm_bias: float32 [640], replicated, may hold values from -4 to 4
- shift_fwd: int32 [80], replicated, may hold values from 0 to 639, as said below
- shift_bwd: int32 [80], replicated, may hold values from 0 to 639, as said below
Outputs:
- in_grad: bfloat16 [2, 256, 16, 16, 640], P('dp', 'frames')
- weight_grad: float32 [640, 5760], P('frames')
- gain_grad: float32 [640], replicated
- bias_grad: float32 [640], replicated
Inputs may be any that keep to these rules, and one draw needn't show every extreme that they name: `shift_fwd`: 80 distinct channel numbers, none of them in shift_bwd. `shift_bwd`: 80 distinct channel numbers, none of them in shift_fwd.
All inputs are finite; a program needn't handle non-finite values.
Results may differ from a plain program's by a relative error of at most 0.003.
Values may be sent and summed in bfloat16 or wider, within the bound.
A program may use at most 128 MiB of HBM per device.

v0:
```python
import jax
import jax.numpy as jnp
from jax import lax
from jax.sharding import PartitionSpec as P

GROUP_CH = 20
epsilon = 1e-05


def with_halo(x, sides, width):
    for axis, dim in sides:
        size, length = (lax.axis_size(axis), x.shape[dim])
        up = [(i, (i + 1) % size) for i in range(size - 1)]
        down = [(j, i) for i, j in up]
        last = lax.slice_in_dim(x, length - width, length, axis=dim)
        first = lax.slice_in_dim(x, 0, width, axis=dim)
        before = lax.ppermute(last, axis, up)
        after = lax.ppermute(first, axis, down)
        x = jnp.concatenate([before, x, after], axis=dim)
    return x


def pad_space(values):
    return jnp.pad(values, ((0, 0), (1, 1), (1, 1), (0, 0)))


def on_device(shifted, out_grad, conv_weight, norm_gain, norm_bias, shift_fwd, shift_bwd):
    frames_local = shifted[0]
    grad_local = out_grad[0]
    frame_count, row_count, col_count, channels = frames_local.shape
    groups = channels // GROUP_CH
    whole_weight = lax.all_gather(conv_weight, "frames", axis=0, tiled=True)
    values = frames_local.astype(jnp.float32).reshape(
        frame_count, row_count * col_count, groups, GROUP_CH
    )
    center = jnp.mean(values, axis=(1, 3), keepdims=True)
    spread = jnp.mean(jnp.square(values - center), axis=(1, 3), keepdims=True)
    inverse = lax.rsqrt(spread + epsilon)
    grouped_normed = (values - center) * inverse
    normed = grouped_normed.reshape(frame_count, row_count, col_count, channels)
    before = normed * norm_gain + norm_bias
    activation = jax.nn.silu(before).astype(jnp.bfloat16)
    act_padded = pad_space(activation)
    grad_padded = pad_space(grad_local)
    grad_rows = grad_local.reshape(-1, channels)
    act_grad = jnp.zeros((grad_rows.shape[0], channels), jnp.float32)
    for tap_index in range(9):
        row_off, col_off = divmod(tap_index, 3)
        grad_view = grad_padded[
            :, 2 - row_off : 2 - row_off + row_count, 2 - col_off : 2 - col_off + col_count, :
        ].reshape(-1, channels)
        act_grad = act_grad + jnp.dot(
            grad_view,
            whole_weight[:, tap_index * channels : (tap_index + 1) * channels],
            preferred_element_type=jnp.float32,
        )
    scale = float(
        lax.axis_size("dp") * lax.axis_size("frames") * frame_count * row_count * col_count
    ) ** (-0.5)
    parts = []
    for tap_index in range(9):
        row_off, col_off = divmod(tap_index, 3)
        act_view = act_padded[
            :, row_off : row_off + row_count, col_off : col_off + col_count, :
        ].reshape(-1, channels)
        parts.append(
            lax.dot_general(
                grad_rows, act_view, (((0,), (0,)), ((), ())), preferred_element_type=jnp.float32
            )
        )
    kernel_shard = lax.psum_scatter(
        jnp.concatenate(parts, axis=1), "frames", scatter_dimension=0, tiled=True
    )
    kernel_shard = lax.psum(kernel_shard, "dp")
    weight_grad = kernel_shard * scale
    sigmoid_val = jax.nn.sigmoid(before)
    pre_grad = act_grad.reshape(before.shape) * sigmoid_val * (1.0 + before * (1.0 - sigmoid_val))
    gain_part = jnp.sum(pre_grad * normed, axis=(0, 1, 2))
    bias_part = jnp.sum(pre_grad, axis=(0, 1, 2))
    gain_total, bias_total = lax.psum((gain_part, bias_part), ("frames", "dp"))
    norm_grad = (pre_grad * norm_gain).reshape(values.shape)
    first_mean = jnp.mean(norm_grad, axis=(1, 3), keepdims=True)
    second_mean = jnp.mean(norm_grad * grouped_normed, axis=(1, 3), keepdims=True)
    shifted_grad = (
        ((norm_grad - first_mean - grouped_normed * second_mean) * inverse)
        .reshape(frames_local.shape)
        .astype(jnp.bfloat16)
    )
    channel_ids = jnp.arange(channels, dtype=jnp.int32)
    forward_match = channel_ids[None, :] == shift_fwd[:, None]
    backward_match = channel_ids[None, :] == shift_bwd[:, None]
    forward_select = forward_match.astype(jnp.bfloat16)
    backward_select = backward_match.astype(jnp.bfloat16)
    forward_mask = jnp.any(forward_match, axis=0)
    backward_mask = jnp.any(backward_match, axis=0)
    plane = row_count * col_count
    first_frame = shifted_grad[0].reshape(plane, channels)
    last_frame = shifted_grad[frame_count - 1].reshape(plane, channels)
    contract_channels = (((1,), (1,)), ((), ()))
    rim_first = lax.dot_general(
        forward_select, first_frame, contract_channels, preferred_element_type=jnp.float32
    ).astype(jnp.bfloat16)
    rim_last = lax.dot_general(
        backward_select, last_frame, contract_channels, preferred_element_type=jnp.float32
    ).astype(jnp.bfloat16)
    extended = with_halo(jnp.stack([rim_first, rim_last]), (("frames", 0),), 1)
    contract_fold = (((0,), (0,)), ((), ()))
    from_prev = lax.dot_general(
        extended[0], backward_select, contract_fold, preferred_element_type=jnp.float32
    ).astype(jnp.bfloat16)
    from_next = lax.dot_general(
        extended[3], forward_select, contract_fold, preferred_element_type=jnp.float32
    ).astype(jnp.bfloat16)
    from_prev = from_prev.reshape(1, row_count, col_count, channels)
    from_next = from_next.reshape(1, row_count, col_count, channels)
    later = jnp.concatenate([shifted_grad[1:], from_next], axis=0)
    earlier = jnp.concatenate([from_prev, shifted_grad[:-1]], axis=0)
    in_grad = jnp.where(forward_mask, later, jnp.where(backward_mask, earlier, shifted_grad))
    return (in_grad[None], weight_grad, gain_total * scale, bias_total * scale)


def solution(mesh):
    in_specs = (
        P("dp", "frames", None, None, None),
        P("dp", "frames", None, None, None),
        P("frames", None),
        P(),
        P(),
        P(),
        P(),
    )
    out_specs = (P("dp", "frames", None, None, None), P("frames", None), P(), P())
    return jax.shard_map(
        on_device, mesh=mesh, in_specs=in_specs, out_specs=out_specs, check_vma=False
    )
```

profile of v0, /device:TPU:1, one launch (start us, length us, event | category | flops | bytes accessed | tf_op | source)
XLA Modules:
  0.0 923.6 jit_solution(15676079137542957894)
XLA Ops:
  7.2 0.7 all-gather.3.cloned.1.call-update
  8.0 21.9 %reshape.226 = f32[4,256,32,20]{3,2,1,0:T(8,128)} reshape(bf16[1,4,16,16,640]{4,3,2,1,0:T(8,128)(2,1)} %param.7) | data formatting | bytes 3932160 | tf_op jit(solution)/shard_map/convert_element_type | solution.py:33
  30.6 0.4 multiply_reduce_fusion.2
  31.5 11.5 %copy.33 = f32[4,256,32,20]{1,0,3,2:T(4,128)} copy(f32[4,256,32,20]{3,2,1,0:T(8,128)} %reshape.226) | data formatting | bytes 5242880 | tf_op jit(solution)/shard_map/convert_element_type | solution.py:33
  43.2 8.8 pad_slice_fusion.8
  52.0 78.7 %all-gather.3.cloned.1.call-done = bf16[64,10,5760]{2,1,0:T(8,128)(2,1)} async-done(((bf16[1,10,5760]{2,1,0:T(8,128)(2,1)}), bf16[64,10,5760]{2,1,0:T(8,128)(2,1)}) %all-gather.3.cloned.1.call-update) | async-done | bytes 7372816 | tf_op jit(solution)/shard_map/all_gather | solution.py:32
  130.7 13.8 %reshape.229 = bf16[640,5760]{1,0:T(8,128)(2,1)} reshape(bf16[64,10,5760]{2,1,0:T(8,128)(2,1)} %all-gather.3.cloned.1.call-done) | data formatting | bytes 14745600
  144.6 3.0 fusion.4
  147.6 0.7 copy-done.1
  148.3 0.3 copy-done.11
  148.6 1.3 fusion.6
  149.9 1.3 fusion.8
  151.3 1.3 fusion.10
  152.6 1.3 fusion.12
  154.0 1.3 fusion.14
  155.3 2.8 fusion.18
  158.1 2.8 fusion.16
  160.9 6.2 fusion.28
  167.1 3.3 copy.31
  170.3 4.2 reshape.215
  174.5 16.5 %fusion.29 = (f32[4,32]{0,1:T(8,128)S(1)}, f32[4,32]{0,1:T(8,128)S(1)}) fusion(f32[4,32]{0,1:T(8,128)S(1)} %copy.34, f32[4,256,32,20]{1,0,3,2:T(4,128)} %copy.33, f32[4,32]{0,1:T(8,128)S(1)} %copy.32, f32[4,256,32,20]{1,0,3,2:T(4,128)} %reshape.215, f32[32,20]{1,0:T(8,128)S(1)} %add.134, f32[32,20]{1,0:T(8,128)S(1)} %mul.201), kind=kLoop, calls=%fused_computation.88 | loop fusion | flops 10485504 | bytes 5250048 | tf_op jit(solution)/shard_map/reduce_sum | solution.py:82
  191.6 3.6 multiply_convert_fusion
  195.2 3.0 pad_slice_fusion
  198.2 2.4 bitcast_dynamic-update-slice_fusion.8
  200.6 2.4 bitcast_dynamic-update-slice_fusion.7
  203.0 2.4 bitcast_dynamic-update-slice_fusion.6
  205.5 2.4 bitcast_dynamic-update-slice_fusion.5
  207.9 2.4 bitcast_dynamic-update-slice_fusion.4
  210.3 2.4 bitcast_dynamic-update-slice_fusion.3
  212.7 2.5 bitcast_dynamic-update-slice_fusion.2
  215.2 2.4 bitcast_dynamic-update-slice_fusion.1
  217.6 2.4 bitcast_dynamic-update-slice_fusion
  220.1 0.6 copy-done.16
  220.7 0.6 dynamic-slice
  222.4 2.2 collective-permute-start
  224.9 3.4 collective-permute-start.1
  228.2 67.9 %all-reduce.3 = (f32[640]{0:T(1024)S(1)}, f32[640]{0:T(1024)S(1)}) all-reduce(f32[640]{0:T(1024)S(1)} %get-tuple-element.25, f32[640]{0:T(1024)S(1)} %get-tuple-element.24), channel_id=1, replica_groups=mesh['frames'=64,'dp'=2] {'frames','dp'}, use_global_device_ids=true, to_apply=%region_11.12 | all-reduce | flops 1280 | bytes 10240 | tf_op jit(solution)/shard_map/psum | solution.py:80
  296.1 1.5 slice_bitcast_fusion
  297.6 0.6 broadcast_multiply_fusion.1
  298.2 1.0 convolution_convert_fusion.1
  299.2 1.0 convolution_convert_fusion
  300.3 516.5 %all-reduce.9.cloned.1.call-done = f32[640,5760]{0,1:T(8,128)} async-done(((f32[640,5760]{0,1:T(8,128)}), f32[640,5760]{0,1:T(8,128)}) %all-reduce.9.cloned.1.call-update) | async-done | bytes 14745616
  816.7 5.1 constant_dynamic-slice_fusion
  821.8 1.2 copy-done.2
  823.3 4.4 maximum_select_fusion
  827.7 82.4 %all-reduce.7.cloned.1.call-done = f32[10,5760]{0,1:T(8,128)} async-done(((f32[10,5760]{0,1:T(8,128)}), f32[10,5760]{0,1:T(8,128)}) %all-reduce.7.cloned.1.call-update) | async-done | bytes 230416 | tf_op jit(solution)/shard_map/psum | solution.py:74
  910.1 3.7 broadcast_multiply_fusion
  913.8 3.0 copy.37
  (64 shorter events, 3.1 us)
Async XLA Ops:
  7.2 123.5 %all-gather.3.cloned.1.call-start = ((), (), s32[]{:S(2)}) async-start(), calls=%async_computation.1 | async-start | bytes 11980800 | tf_op jit(solution)/shard_map/all_gather | solution.py:32
  7.9 22.0 %copy-start = (bf16[1,4,16,16,640]{4,3,2,1,0:T(8,128)(2,1)S(1)}, bf16[1,4,16,16,640]{4,3,2,1,0:T(8,128)(2,1)}, u32[]{:S(2)}) copy-start(bf16[1,4,16,16,640]{4,3,2,1,0:T(8,128)(2,1)} %param.7) | copy-start | bytes 3932164
  7.9 808.8 %all-reduce.9.cloned.1.call-start = ((), (), s32[]{:S(2)}) async-start(), calls=%async_computation.2 | async-start | bytes 29491200
  31.5 11.5 %copy-start.12 = (f32[640]{0:T(1024)S(1)}, f32[640]{0:T(1024)}, u32[]{:S(2)}) copy-start(f32[640]{0:T(1024)} %param.11) | copy-start | bytes 7684
  31.5 11.6 %copy-start.13 = (f32[640]{0:T(1024)S(1)}, f32[640]{0:T(1024)}, u32[]{:S(2)}) copy-start(f32[640]{0:T(1024)} %param.10) | copy-start | bytes 7684
  144.5 3.7 copy-start.1
  144.6 4.0 copy-start.11
  148.6 1.3 copy-start.10
  149.9 1.3 copy-start.4
  151.3 1.3 copy-start.9
  152.6 1.3 copy-start.8
  154.0 1.3 copy-start.7
  155.3 2.8 copy-start.6
  195.2 3.0 copy-start.5
  220.1 0.7 copy-start.16
  220.1 1.9 copy-start.14
  220.1 1.9 copy-start.15
  220.1 690.0 %all-reduce.7.cloned.1.call-start = ((), (), s32[]{:S(2)}) async-start(), calls=%async_computation | async-start | bytes 5898240 | tf_op jit(solution)/shard_map/psum | solution.py:74
  222.4 75.8 %collective-permute-start = (bf16[1,80,256]{2,1,0:T(8,128)(2,1)S(1)}, bf16[1,80,256]{2,1,0:T(8,128)(2,1)S(1)}, u32[]{:S(2)}, u32[]{:S(2)}) collective-permute-start(bf16[1,80,256]{2,1,0:T(8,128)(2,1)S(1)} %fusion.1), channel_id=1, source_target_pairs={{2,0},{4,2},{6,4},{8,6},{10,8},{12,10},{14,12},{16,14},{18,16},{20... | collective-permute-start | bytes 122888 | tf_op jit(solution)/shard_map/ppermute | solution.py:18
  224.9 74.4 %collective-permute-start.1 = (bf16[1,80,256]{2,1,0:T(8,128)(2,1)S(1)}, bf16[1,80,256]{2,1,0:T(8,128)(2,1)S(1)}, u32[]{:S(2)}, u32[]{:S(2)}) collective-permute-start(bf16[1,80,256]{2,1,0:T(8,128)(2,1)S(1)} %fusion.2), channel_id=1, source_target_pairs={{0,2},{2,4},{4,6},{6,8},{8,10},{10,12},{12,14},{14,16},{16,18},{18... | collective-permute-start | bytes 122888 | tf_op jit(solution)/shard_map/ppermute | solution.py:17
  821.8 1.2 copy-start.2
  821.8 1.5 copy-start.3
Sparse Core Ops, SparseCore 0:
  9.7 120.9 all-gather.2
  220.2 596.4 all-reduce.8
  822.0 88.0 all-reduce.6
where the time goes:
time: 929 us; the launch traced here: 924 us
  waiting for transfers between devices  678 us (73%)
  local copies, waits for them, and re-layouts  81.4 us (9%)
  blocking collectives  67.9 us (7%)
  matrix products  45.7 us (5%)
  other arithmetic  29.7 us (3%)
  between operations  15 us (2%)
    unnamed x4, waiting for transfers between devices  517 us
    psum x1, waiting for transfers between devices, on_device(): kernel_shard = lax.psum(kernel_shard, 'dp')  82.4 us
    all_gather x1, waiting for transfers between devices, on_device(): whole_weight = lax.all_gather(conv_weight, 'frames', axis=0, tiled=True)  78.7 us
    psum x1, blocking collectives, on_device(): gain_total, bias_total = lax.psum((gain_part, bias_part), ('frames', 'dp'))  67.9 us
    convert_element_type x2, local copies, waits for them, and re-layouts, on_device(): frames_local.astype(jnp.float32)  33.4 us
    unnamed x38, local copies, waits for them, and re-layouts  25.6 us
    dot_general x9, matrix products, on_device(): lax.dot_general(grad_rows, act_view, (((0,), (0,)), ((), ())), preferred_...  21.8 us
    dot_general x9, matrix products, on_device(): jnp.dot(grad_view, whole_weight[:, tap_index * channels:(tap_index + 1) *...  21.3 us
  transfers between devices with their start and end apart: 5, of which 3 were waited for; matrix products, arithmetic and copies ran while one was open for 6% of the time, Pallas kernels for 0%

commit v1 on v0

--- a/solution.py
+++ b/solution.py
@@ -2,6 +2,7 @@
 import jax.numpy as jnp
 from jax import lax
 from jax.sharding import PartitionSpec as P
+from jax.lax import psum
 
 GROUP_CH = 20
 epsilon = 1e-05
@@ -77,7 +78,7 @@
     pre_grad = act_grad.reshape(before.shape) * sigmoid_val * (1.0 + before * (1.0 - sigmoid_val))
     gain_part = jnp.sum(pre_grad * normed, axis=(0, 1, 2))
     bias_part = jnp.sum(pre_grad, axis=(0, 1, 2))
-    gain_total, bias_total = lax.psum((gain_part, bias_part), ("frames", "dp"))
+    gain_total, bias_total = psum(psum((gain_part, bias_part), "dp"), "frames")
     norm_grad = (pre_grad * norm_gain).reshape(values.shape)
     first_mean = jnp.mean(norm_grad, axis=(1, 3), keepdims=True)
     second_mean = jnp.mean(norm_grad * grouped_normed, axis=(1, 3), keepdims=True)

time: 929 us -> 915 us (0.985)
  blocking collectives: 67.9 us -> 146 us
  waiting for transfers between devices: 678 us -> 602 us
  other arithmetic: 29.7 us -> 18.9 us
    psum x1 -> x2, blocking collectives: 67.9 us -> 146 us  [on_device(): gain_total, bias_total = psum(psum((gain_part, bias_part), 'dp'), 'frames')]
    unnamed x4, waiting for transfers between devices: 517 us -> 441 us
    reduce_sum x1, other arithmetic: 16.5 us -> 5.68 us  [on_device(): first_mean = jnp.mean(norm_grad, axis=(1, 3), keepdims=True)]
where the time goes in v1:
time: 915 us; the launch traced here: 914 us
  waiting for transfers between devices  602 us (66%)
  blocking collectives  146 us (16%)
  local copies, waits for them, and re-layouts  81 us (9%)
  matrix products  45.7 us (5%)
  other arithmetic  18.9 us (2%)
  between operations  14.7 us (2%)
    unnamed x4, waiting for transfers between devices  441 us
    psum x2, blocking collectives, on_device(): gain_total, bias_total = psum(psum((gain_part, bias_part), 'dp'), 'frames')  146 us
    psum x1, waiting for transfers between devices, on_device(): kernel_shard = lax.psum(kernel_shard, 'dp')  82.4 us
    all_gather x1, waiting for transfers between devices, on_device(): whole_weight = lax.all_gather(conv_weight, 'frames', axis=0, tiled=True)  78.7 us
    convert_element_type x2, local copies, waits for them, and re-layouts, on_device(): frames_local.astype(jnp.float32)  33.4 us
    unnamed x38, local copies, waits for them, and re-layouts  25.3 us
    dot_general x9, matrix products, on_device(): lax.dot_general(grad_rows, act_view, (((0,), (0,)), ((), ())), preferred_...  21.8 us
    dot_general x9, matrix products, on_device(): jnp.dot(grad_view, whole_weight[:, tap_index * channels:(tap_index + 1) *...  21.3 us
  transfers between devices with their start and end apart: 5, of which 3 were waited for; matrix products, arithmetic and copies ran while one was open for 6% of the time, Pallas kernels for 0%

profile of v1, /device:TPU:1, one launch (start us, length us, event | category | flops | bytes accessed | tf_op | source)
XLA Modules:
  0.0 914.2 jit_solution(15801352893657435228)
XLA Ops:
  7.2 0.7 all-gather.3.cloned.1.call-update
  8.0 21.9 %reshape.226 = f32[4,256,32,20]{3,2,1,0:T(8,128)} reshape(bf16[1,4,16,16,640]{4,3,2,1,0:T(8,128)(2,1)} %param.7) | data formatting | bytes 3932160 | tf_op jit(solution)/shard_map/convert_element_type | solution.py:34
  30.6 0.4 multiply_reduce_fusion.2
  31.5 11.5 %copy.33 = f32[4,256,32,20]{1,0,3,2:T(4,128)} copy(f32[4,256,32,20]{3,2,1,0:T(8,128)} %reshape.226) | data formatting | bytes 5242880 | tf_op jit(solution)/shard_map/convert_element_type | solution.py:34
  43.2 8.8 pad_slice_fusion.8
  52.0 78.7 %all-gather.3.cloned.1.call-done = bf16[64,10,5760]{2,1,0:T(8,128)(2,1)} async-done(((bf16[1,10,5760]{2,1,0:T(8,128)(2,1)}), bf16[64,10,5760]{2,1,0:T(8,128)(2,1)}) %all-gather.3.cloned.1.call-update) | async-done | bytes 7372816 | tf_op jit(solution)/shard_map/all_gather | solution.py:33
  130.7 13.5 %reshape.229 = bf16[640,5760]{1,0:T(8,128)(2,1)} reshape(bf16[64,10,5760]{2,1,0:T(8,128)(2,1)} %all-gather.3.cloned.1.call-done) | data formatting | bytes 14745600
  144.2 3.0 fusion.4
  147.2 0.7 copy-done.1
  148.2 1.3 fusion.6
  149.6 1.3 fusion.8
  150.9 1.3 fusion.10
  152.3 1.3 fusion.12
  153.6 1.3 fusion.14
  155.0 2.8 fusion.18
  157.7 2.8 fusion.16
  160.6 6.2 fusion.28
  166.7 3.3 copy.31
  170.0 4.2 reshape.215
  174.2 5.7 fusion.29
  180.4 3.6 multiply_convert_fusion
  184.0 3.0 pad_slice_fusion
  187.0 2.4 bitcast_dynamic-update-slice_fusion.8
  189.4 2.4 bitcast_dynamic-update-slice_fusion.7
  191.9 2.4 bitcast_dynamic-update-slice_fusion.6
  194.3 2.4 bitcast_dynamic-update-slice_fusion.5
  196.7 2.4 bitcast_dynamic-update-slice_fusion.4
  199.1 2.4 bitcast_dynamic-update-slice_fusion.3
  201.5 2.5 bitcast_dynamic-update-slice_fusion.2
  204.0 2.4 bitcast_dynamic-update-slice_fusion.1
  206.5 2.4 bitcast_dynamic-update-slice_fusion
  209.0 0.6 copy-done.16
  209.5 0.6 dynamic-slice
  211.2 2.2 collective-permute-start
  213.7 3.4 collective-permute-start.1
  217.1 5.9 all-reduce.4
  223.0 140.5 %all-reduce.3 = (f32[640]{0:T(1024)S(1)}, f32[640]{0:T(1024)S(1)}) all-reduce(f32[640]{0:T(1024)S(1)} %get-tuple-element.30, f32[640]{0:T(1024)S(1)} %get-tuple-element.31), channel_id=1, replica_groups=mesh['frames'=64,'dp'=2] {'frames'}, use_global_device_ids=true, to_apply=%region_12.13 | all-reduce | flops 1280 | bytes 10240 | tf_op jit(solution)/shard_map/psum | solution.py:81
  363.5 1.5 slice_bitcast_fusion
  365.0 0.6 broadcast_multiply_fusion.1
  365.6 1.0 convolution_convert_fusion.1
  366.6 1.0 convolution_convert_fusion
  367.6 439.9 %all-reduce.10.cloned.1.call-done = f32[640,5760]{0,1:T(8,128)} async-done(((f32[640,5760]{0,1:T(8,128)}), f32[640,5760]{0,1:T(8,128)}) %all-reduce.10.cloned.1.call-update) | async-done | bytes 14745616
  807.6 5.1 constant_dynamic-slice_fusion
  812.7 1.2 copy-done.2
  814.1 4.4 maximum_select_fusion
  818.5 82.4 %all-reduce.8.cloned.1.call-done = f32[10,5760]{0,1:T(8,128)} async-done(((f32[10,5760]{0,1:T(8,128)}), f32[10,5760]{0,1:T(8,128)}) %all-reduce.8.cloned.1.call-update) | async-done | bytes 230416 | tf_op jit(solution)/shard_map/psum | solution.py:75
  900.9 3.7 broadcast_multiply_fusion
  904.6 3.0 copy.37
  (65 shorter events, 3.4 us)
Async XLA Ops:
  7.2 123.5 %all-gather.3.cloned.1.call-start = ((), (), s32[]{:S(2)}) async-start(), calls=%async_computation.1 | async-start | bytes 11980800 | tf_op jit(solution)/shard_map/all_gather | solution.py:33
  7.9 22.0 %copy-start = (bf16[1,4,16,16,640]{4,3,2,1,0:T(8,128)(2,1)S(1)}, bf16[1,4,16,16,640]{4,3,2,1,0:T(8,128)(2,1)}, u32[]{:S(2)}) copy-start(bf16[1,4,16,16,640]{4,3,2,1,0:T(8,128)(2,1)} %param.7) | copy-start | bytes 3932164
  7.9 799.7 %all-reduce.10.cloned.1.call-start = ((), (), s32[]{:S(2)}) async-start(), calls=%async_computation.2 | async-start | bytes 29491200
  31.5 11.5 %copy-start.12 = (f32[640]{0:T(1024)S(1)}, f32[640]{0:T(1024)}, u32[]{:S(2)}) copy-start(f32[640]{0:T(1024)} %param.11) | copy-start | bytes 7684
  31.5 11.6 %copy-start.13 = (f32[640]{0:T(1024)S(1)}, f32[640]{0:T(1024)}, u32[]{:S(2)}) copy-start(f32[640]{0:T(1024)} %param.10) | copy-start | bytes 7684
  144.2 3.7 copy-start.1
  144.2 4.1 copy-start.11
  148.2 1.3 copy-start.10
  149.6 1.3 copy-start.4
  150.9 1.3 copy-start.9
  152.3 1.3 copy-start.8
  153.6 1.3 copy-start.7
  154.9 2.8 copy-start.6
  184.0 3.0 copy-start.5
  208.9 0.7 copy-start.16
  208.9 1.9 copy-start.14
  208.9 1.9 copy-start.15
  208.9 692.0 %all-reduce.8.cloned.1.call-start = ((), (), s32[]{:S(2)}) async-start(), calls=%async_computation | async-start | bytes 5898240 | tf_op jit(solution)/shard_map/psum | solution.py:75
  211.2 154.3 %collective-permute-start = (bf16[1,80,256]{2,1,0:T(8,128)(2,1)S(1)}, bf16[1,80,256]{2,1,0:T(8,128)(2,1)S(1)}, u32[]{:S(2)}, u32[]{:S(2)}) collective-permute-start(bf16[1,80,256]{2,1,0:T(8,128)(2,1)S(1)} %fusion.1), channel_id=1, source_target_pairs={{2,0},{4,2},{6,4},{8,6},{10,8},{12,10},{14,12},{16,14},{18,16},{20... | collective-permute-start | bytes 122888 | tf_op jit(solution)/shard_map/ppermute | solution.py:19
  213.7 152.9 %collective-permute-start.1 = (bf16[1,80,256]{2,1,0:T(8,128)(2,1)S(1)}, bf16[1,80,256]{2,1,0:T(8,128)(2,1)S(1)}, u32[]{:S(2)}, u32[]{:S(2)}) collective-permute-start(bf16[1,80,256]{2,1,0:T(8,128)(2,1)S(1)} %fusion.2), channel_id=1, source_target_pairs={{0,2},{2,4},{4,6},{6,8},{8,10},{10,12},{12,14},{14,16},{16,18},{18... | collective-permute-start | bytes 122888 | tf_op jit(solution)/shard_map/ppermute | solution.py:18
  812.6 1.2 copy-start.2
  812.6 1.5 copy-start.3
Sparse Core Ops, SparseCore 0:
  9.7 120.9 all-gather.2
  209.0 598.4 all-reduce.9
  812.8 88.0 all-reduce.7
